TPU v7x, 32 devices: a whole 2x2x4 slice. The times are simulated.
32 devices in a mesh: dp: 8 (over z, y), fsdp: 4 (over x, core).
Axes of the slice: x: 2, y: 2, z: 4, core: 2. Of those that a mesh axis runs over, the one named last changes fastest.
Arguments:
- tokens: bfloat16 [6144, 768], P(('dp', 'fsdp')), may hold values from -6 to 6
- lengths: int32 [32, 4], P(('dp', 'fsdp')), may hold values from 1 to 168, 192 in all within a row
- cotangent: bfloat16 [6144, 768], P(('dp', 'fsdp')), may hold values from -6 to 6
- w_qkv: bfloat16 [768, 2304], P(('dp', 'fsdp')), may hold values from -0.21875 to 0.21875
- bias_q: bfloat16 [768], P(('dp', 'fsdp')), may hold values from -3 to 3
- bias_v: bfloat16 [768], P(('dp', 'fsdp')), may hold values from -3 to 3
- w_out: bfloat16 [768, 768], P(('dp', 'fsdp')), may hold values from -0.625 to 0.625
- bias_out: bfloat16 [768], P(('dp', 'fsdp')), may hold values from -2 to 2
- gain_attn: bfloat16 [768], P(('dp', 'fsdp')), may hold values from 0.25 to 1.75
- shift_attn: bfloat16 [768], P(('dp', 'fsdp')), may hold values from -2 to 2
- gain_mlp: bfloat16 [768], P(('dp', 'fsdp')), may hold values from 0.25 to 1.75
- shift_mlp: bfloat16 [768], P(('dp', 'fsdp')), may hold values from -2 to 2
- w_up: bfloat16 [768, 3072], P(('dp', 'fsdp')), may hold values from -0.21875 to 0.21875
- bias_up: bfloat16 [3072], P(('dp', 'fsdp')), may hold values from -2 to 2
- w_down: bfloat16 [3072, 768], P(('dp', 'fsdp')), may hold values from -0.109375 to 0.109375
- bias_down: bfloat16 [768], P(('dp', 'fsdp')), may hold values from -2 to 2
- pass_embed: bfloat16 [3, 768], P(None, ('dp', 'fsdp')), may hold values from -3 to 3
Outputs:
- output: bfloat16 [6144, 768], P(('dp', 'fsdp'))
- token_grad: bfloat16 [6144, 768], P(('dp', 'fsdp'))
- grad_w_qkv: float32 [768, 2304], P(('dp', 'fsdp'))
- grad_bias_q: float32 [768], P(('dp', 'fsdp'))
- grad_bias_v: float32 [768], P(('dp', 'fsdp'))
- grad_w_out: float32 [768, 768], P(('dp', 'fsdp'))
- grad_bias_out: float32 [768], P(('dp', 'fsdp'))
- grad_gain_attn: float32 [768], P(('dp', 'fsdp'))
- grad_shift_attn: float32 [768], P(('dp', 'fsdp'))
- grad_gain_mlp: float32 [768], P(('dp', 'fsdp'))
- grad_shift_mlp: float32 [768], P(('dp', 'fsdp'))
- grad_w_up: float32 [768, 3072], P(('dp', 'fsdp'))
- grad_bias_up: float32 [3072], P(('dp', 'fsdp'))
- grad_w_down: float32 [3072, 768], P(('dp', 'fsdp'))
- grad_bias_down: float32 [768], P(('dp', 'fsdp'))
- grad_pass_embed: float32 [3, 768], P(None, ('dp', 'fsdp'))
Inputs may be any that keep to these rules, and one draw needn't show every extreme that they name: The 4 lengths of each row sum to 192; in every row the longest is exactly 168.
All inputs are finite; a program needn't handle non-finite values.
Results may differ from a plain program's by a relative error of at most 0.015.
Values may be sent and summed in bfloat16 or wider, within the bound.
No kernel may reach another device: no remote copies, remote signals or barrier semaphores. Data moves between devices by JAX's collectives and lax.ppermute only.
A program may use at most 192 MiB of HBM per device.

v0:
```python
import jax
import jax.numpy as jnp
from jax import lax
from jax.sharding import PartitionSpec as P

HEAD_DIM = 64
PASSES = 3


EPSILON = 1e-05


def layer_norm(values, gain_vec, shift_vec):
    average = jnp.mean(values, axis=-1, keepdims=True)
    centred = values - average
    spread = jnp.mean(centred * centred, axis=-1, keepdims=True)
    return centred * lax.rsqrt(spread + EPSILON) * gain_vec + shift_vec


def gelu_tanh(values):
    return jax.nn.gelu(values, approximate=True)


def fetch_once(
    w_qkv,
    bias_q,
    bias_v,
    w_out,
    bias_out,
    gain_attn,
    shift_attn,
    gain_mlp,
    shift_mlp,
    w_up,
    bias_up,
    w_down,
    bias_down,
    pass_embed,
):
    return (
        lax.all_gather(w_qkv, ("dp", "fsdp"), axis=0, tiled=True),
        lax.all_gather(bias_q, ("dp", "fsdp"), axis=0, tiled=True),
        lax.all_gather(bias_v, ("dp", "fsdp"), axis=0, tiled=True),
        lax.all_gather(w_out, ("dp", "fsdp"), axis=0, tiled=True),
        lax.all_gather(bias_out, ("dp", "fsdp"), axis=0, tiled=True),
        lax.all_gather(gain_attn, ("dp", "fsdp"), axis=0, tiled=True),
        lax.all_gather(shift_attn, ("dp", "fsdp"), axis=0, tiled=True),
        lax.all_gather(gain_mlp, ("dp", "fsdp"), axis=0, tiled=True),
        lax.all_gather(shift_mlp, ("dp", "fsdp"), axis=0, tiled=True),
        lax.all_gather(w_up, ("dp", "fsdp"), axis=0, tiled=True),
        lax.all_gather(bias_up, ("dp", "fsdp"), axis=0, tiled=True),
        lax.all_gather(w_down, ("dp", "fsdp"), axis=0, tiled=True),
        lax.all_gather(bias_down, ("dp", "fsdp"), axis=0, tiled=True),
        lax.all_gather(pass_embed, ("dp", "fsdp"), axis=1, tiled=True),
    )


def reduce_total(grad_set):
    return (
        lax.psum_scatter(grad_set[0], ("dp", "fsdp"), scatter_dimension=0, tiled=True),
        lax.psum_scatter(grad_set[1], ("dp", "fsdp"), scatter_dimension=0, tiled=True),
        lax.psum_scatter(grad_set[2], ("dp", "fsdp"), scatter_dimension=0, tiled=True),
        lax.psum_scatter(grad_set[3], ("dp", "fsdp"), scatter_dimension=0, tiled=True),
        lax.psum_scatter(grad_set[4], ("dp", "fsdp"), scatter_dimension=0, tiled=True),
        lax.psum_scatter(grad_set[5], ("dp", "fsdp"), scatter_dimension=0, tiled=True),
        lax.psum_scatter(grad_set[6], ("dp", "fsdp"), scatter_dimension=0, tiled=True),
        lax.psum_scatter(grad_set[7], ("dp", "fsdp"), scatter_dimension=0, tiled=True),
        lax.psum_scatter(grad_set[8], ("dp", "fsdp"), scatter_dimension=0, tiled=True),
        lax.psum_scatter(grad_set[9], ("dp", "fsdp"), scatter_dimension=0, tiled=True),
        lax.psum_scatter(grad_set[10], ("dp", "fsdp"), scatter_dimension=0, tiled=True),
        lax.psum_scatter(grad_set[11], ("dp", "fsdp"), scatter_dimension=0, tiled=True),
        lax.psum_scatter(grad_set[12], ("dp", "fsdp"), scatter_dimension=0, tiled=True),
        lax.psum_scatter(grad_set[13], ("dp", "fsdp"), scatter_dimension=1, tiled=True),
    )


def masked_scores(queries, key_stack, allowed):
    length, model_width = queries.shape
    head_count = model_width // HEAD_DIM
    query_heads = queries.reshape(length, head_count, HEAD_DIM)
    key_heads = key_stack.reshape(-1, head_count, HEAD_DIM)
    raw_scores = jnp.einsum(
        "thd,shd->hts", query_heads, key_heads, preferred_element_type=jnp.float32
    ) * HEAD_DIM ** (-0.5)
    return (jnp.where(allowed[None], raw_scores, -1e30), query_heads, key_heads)


def attend_forward(queries, key_stack, value_stack, allowed):
    length, model_width = queries.shape
    head_count = model_width // HEAD_DIM
    masked, query_heads, key_heads = masked_scores(queries, key_stack, allowed)
    row_top = jnp.max(masked, axis=-1, keepdims=True)
    weights = jnp.exp(masked - row_top)
    row_total = jnp.sum(weights, axis=-1, keepdims=True)
    prob_low = (weights / row_total).astype(jnp.bfloat16)
    value_heads = value_stack.reshape(-1, head_count, HEAD_DIM)
    context = jnp.einsum("hts,shd->thd", prob_low, value_heads, preferred_element_type=jnp.float32)
    return (context.reshape(length, model_width).astype(jnp.bfloat16), row_top + jnp.log(row_total))


def attend_backward(queries, key_stack, value_stack, grad_context, log_total, allowed):
    length, model_width = queries.shape
    head_count = model_width // HEAD_DIM
    masked, query_heads, key_heads = masked_scores(queries, key_stack, allowed)
    prob_full = jnp.exp(masked - log_total)
    value_heads = value_stack.reshape(-1, head_count, HEAD_DIM)
    grad_heads = grad_context.reshape(length, head_count, HEAD_DIM)
    grad_probs = jnp.einsum(
        "thd,shd->hts", grad_heads, value_heads, preferred_element_type=jnp.float32
    )
    row_inner = jnp.sum(prob_full * grad_probs, axis=-1, keepdims=True)
    grad_scores = (prob_full * (grad_probs - row_inner)).astype(jnp.bfloat16)
    score_scale = HEAD_DIM ** (-0.5)
    grad_queries = (
        jnp.einsum("hts,shd->thd", grad_scores, key_heads, preferred_element_type=jnp.float32)
        * score_scale
    )
    grad_keys = (
        jnp.einsum("hts,thd->shd", grad_scores, query_heads, preferred_element_type=jnp.float32)
        * score_scale
    )
    grad_values = jnp.einsum(
        "hts,thd->shd",
        prob_full.astype(jnp.bfloat16),
        grad_heads,
        preferred_element_type=jnp.float32,
    )
    return (
        grad_queries.reshape(length, model_width),
        grad_keys.reshape(-1, model_width),
        grad_values.reshape(-1, model_width),
    )


def forward_pass(residual, gathered, repeat, key_list, value_list, allowed_base):
    (
        w_qkv,
        bias_q,
        bias_v,
        w_out,
        bias_out,
        gain_attn,
        shift_attn,
        gain_mlp,
        shift_mlp,
        w_up,
        bias_up,
        w_down,
        bias_down,
        pass_embed,
    ) = gathered
    model_width = residual.shape[1]
    entry_state = residual + pass_embed[repeat].astype(jnp.float32)
    normed = layer_norm(
        entry_state, gain_attn.astype(jnp.float32), shift_attn.astype(jnp.float32)
    ).astype(jnp.bfloat16)
    qkv_bias = jnp.concatenate(
        [
            bias_q.astype(jnp.float32),
            jnp.zeros((model_width,), jnp.float32),
            bias_v.astype(jnp.float32),
        ]
    )
    mixed_qkv = (jnp.dot(normed, w_qkv, preferred_element_type=jnp.float32) + qkv_bias).astype(
        jnp.bfloat16
    )
    queries = mixed_qkv[:, :model_width]
    key_list.append(mixed_qkv[:, model_width : 2 * model_width])
    value_list.append(mixed_qkv[:, 2 * model_width :])
    allowed = jnp.tile(allowed_base, (1, repeat + 1))
    context, log_total = attend_forward(
        queries, jnp.concatenate(key_list, axis=0), jnp.concatenate(value_list, axis=0), allowed
    )
    middle = entry_state + (
        jnp.dot(context, w_out, preferred_element_type=jnp.float32) + bias_out.astype(jnp.float32)
    )
    normed_mlp = layer_norm(
        middle, gain_mlp.astype(jnp.float32), shift_mlp.astype(jnp.float32)
    ).astype(jnp.bfloat16)
    hidden = jnp.dot(normed_mlp, w_up, preferred_element_type=jnp.float32) + bias_up.astype(
        jnp.float32
    )
    active = gelu_tanh(hidden).astype(jnp.bfloat16)
    residual = middle + (
        jnp.dot(active, w_down, preferred_element_type=jnp.float32) + bias_down.astype(jnp.float32)
    )
    return (residual, (entry_state, queries, context, log_total, middle, hidden))


def backward_pass(
    grad_state,
    gathered,
    repeat,
    saved_pass,
    key_list,
    value_list,
    key_grads,
    value_grads,
    allowed_base,
):
    (
        w_qkv,
        bias_q,
        bias_v,
        w_out,
        bias_out,
        gain_attn,
        shift_attn,
        gain_mlp,
        shift_mlp,
        w_up,
        bias_up,
        w_down,
        bias_down,
        pass_embed,
    ) = gathered
    entry_state, queries, context, log_total, middle, hidden = saved_pass
    length, model_width = queries.shape
    update_grad = grad_state.astype(jnp.bfloat16)
    active, gelu_pull = jax.vjp(gelu_tanh, hidden)
    grad_w_down = jnp.einsum(
        "tf,td->fd", active.astype(jnp.bfloat16), update_grad, preferred_element_type=jnp.float32
    )
    grad_bias_down = jnp.sum(update_grad.astype(jnp.float32), axis=0)
    (grad_hidden,) = gelu_pull(
        jnp.einsum("td,fd->tf", update_grad, w_down, preferred_element_type=jnp.float32)
    )
    grad_hidden = grad_hidden.astype(jnp.bfloat16)
    normed_mlp, mlp_pull = jax.vjp(
        layer_norm, middle, gain_mlp.astype(jnp.float32), shift_mlp.astype(jnp.float32)
    )
    grad_w_up = jnp.einsum(
        "td,tf->df",
        normed_mlp.astype(jnp.bfloat16),
        grad_hidden,
        preferred_element_type=jnp.float32,
    )
    grad_bias_up = jnp.sum(grad_hidden.astype(jnp.float32), axis=0)
    grad_middle, grad_gain_mlp, grad_shift_mlp = mlp_pull(
        jnp.einsum("tf,df->td", grad_hidden, w_up, preferred_element_type=jnp.float32)
    )
    grad_middle = grad_state + grad_middle
    branch_grad = grad_middle.astype(jnp.bfloat16)
    grad_w_out = jnp.einsum("te,td->ed", context, branch_grad, preferred_element_type=jnp.float32)
    grad_bias_out = jnp.sum(branch_grad.astype(jnp.float32), axis=0)
    grad_context = jnp.einsum(
        "td,ed->te", branch_grad, w_out, preferred_element_type=jnp.float32
    ).astype(jnp.bfloat16)
    allowed = jnp.tile(allowed_base, (1, repeat + 1))
    grad_queries, grad_keys, grad_values = attend_backward(
        queries,
        jnp.concatenate(key_list[: repeat + 1], axis=0),
        jnp.concatenate(value_list[: repeat + 1], axis=0),
        grad_context,
        log_total,
        allowed,
    )
    for earlier in range(repeat + 1):
        key_grads[earlier] = (
            key_grads[earlier] + grad_keys[earlier * length : (earlier + 1) * length]
        )
        value_grads[earlier] = (
            value_grads[earlier] + grad_values[earlier * length : (earlier + 1) * length]
        )
    grad_mixed = jnp.concatenate(
        [grad_queries, key_grads[repeat], value_grads[repeat]], axis=1
    ).astype(jnp.bfloat16)
    grad_bias_q = jnp.sum(grad_mixed[:, :model_width].astype(jnp.float32), axis=0)
    grad_bias_v = jnp.sum(grad_mixed[:, 2 * model_width :].astype(jnp.float32), axis=0)
    normed, attn_pull = jax.vjp(
        layer_norm, entry_state, gain_attn.astype(jnp.float32), shift_attn.astype(jnp.float32)
    )
    grad_w_qkv = jnp.einsum(
        "td,te->de", normed.astype(jnp.bfloat16), grad_mixed, preferred_element_type=jnp.float32
    )
    grad_entry, grad_gain_attn, grad_shift_attn = attn_pull(
        jnp.einsum("te,de->td", grad_mixed, w_qkv, preferred_element_type=jnp.float32)
    )
    grad_entry = grad_middle + grad_entry
    grad_embed = (
        jnp.zeros((PASSES, model_width), jnp.float32).at[repeat].set(jnp.sum(grad_entry, axis=0))
    )
    return (
        grad_entry,
        (
            grad_w_qkv,
            grad_bias_q,
            grad_bias_v,
            grad_w_out,
            grad_bias_out,
            grad_gain_attn,
            grad_shift_attn,
            grad_gain_mlp,
            grad_shift_mlp,
            grad_w_up,
            grad_bias_up,
            grad_w_down,
            grad_bias_down,
            grad_embed,
        ),
    )


def per_device(
    tokens,
    lengths,
    cotangent,
    w_qkv,
    bias_q,
    bias_v,
    w_out,
    bias_out,
    gain_attn,
    shift_attn,
    gain_mlp,
    shift_mlp,
    w_up,
    bias_up,
    w_down,
    bias_down,
    pass_embed,
):
    length, model_width = tokens.shape
    position = jnp.arange(length, dtype=jnp.int32)
    doc_ends = jnp.cumsum(lengths[0])
    doc_ids = jnp.sum((position[:, None] >= doc_ends[None, :]).astype(jnp.int32), axis=1)
    allowed_base = (doc_ids[:, None] == doc_ids[None, :]) & (position[None, :] <= position[:, None])
    gathered = fetch_once(
        w_qkv,
        bias_q,
        bias_v,
        w_out,
        bias_out,
        gain_attn,
        shift_attn,
        gain_mlp,
        shift_mlp,
        w_up,
        bias_up,
        w_down,
        bias_down,
        pass_embed,
    )
    residual = tokens.astype(jnp.float32)
    key_list = []
    value_list = []
    saved_list = []
    for repeat in range(PASSES):
        residual, saved_pass = forward_pass(
            residual, gathered, repeat, key_list, value_list, allowed_base
        )
        saved_list.append(saved_pass)
    output = residual.astype(jnp.bfloat16)
    grad_state = cotangent.astype(jnp.float32)
    key_grads = [jnp.zeros((length, model_width), jnp.float32) for repeat in range(PASSES)]
    value_grads = [jnp.zeros((length, model_width), jnp.float32) for repeat in range(PASSES)]
    totals = None
    for repeat in reversed(range(PASSES)):
        grad_state, pass_grads = backward_pass(
            grad_state,
            gathered,
            repeat,
            saved_list[repeat],
            key_list,
            value_list,
            key_grads,
            value_grads,
            allowed_base,
        )
        totals = (
            pass_grads
            if totals is None
            else tuple((running + extra for running, extra in zip(totals, pass_grads)))
        )
    totals = reduce_total(totals)
    return (
        output,
        grad_state.astype(jnp.bfloat16),
        totals[0],
        totals[1],
        totals[2],
        totals[3],
        totals[4],
        totals[5],
        totals[6],
        totals[7],
        totals[8],
        totals[9],
        totals[10],
        totals[11],
        totals[12],
        totals[13],
    )


def solution(mesh):
    placed = (
        P(("dp", "fsdp"), None),
        P(("dp", "fsdp"), None),
        P(("dp", "fsdp"), None),
        P(("dp", "fsdp"), None),
        P(("dp", "fsdp")),
        P(("dp", "fsdp")),
        P(("dp", "fsdp"), None),
        P(("dp", "fsdp")),
        P(("dp", "fsdp")),
        P(("dp", "fsdp")),
        P(("dp", "fsdp")),
        P(("dp", "fsdp")),
        P(("dp", "fsdp"), None),
        P(("dp", "fsdp")),
        P(("dp", "fsdp"), None),
        P(("dp", "fsdp")),
        P(None, ("dp", "fsdp")),
    )
    return jax.shard_map(
        per_device,
        mesh=mesh,
        in_specs=placed,
        out_specs=(
            P(("dp", "fsdp"), None),
            P(("dp", "fsdp"), None),
            P(("dp", "fsdp"), None),
            P(("dp", "fsdp")),
            P(("dp", "fsdp")),
            P(("dp", "fsdp"), None),
            P(("dp", "fsdp")),
            P(("dp", "fsdp")),
            P(("dp", "fsdp")),
            P(("dp", "fsdp")),
            P(("dp", "fsdp")),
            P(("dp", "fsdp"), None),
            P(("dp", "fsdp")),
            P(("dp", "fsdp"), None),
            P(("dp", "fsdp")),
            P(None, ("dp", "fsdp")),
        ),
        check_vma=False,
    )
```

profile of v0, /device:TPU:0, one launch (start us, length us, event | category | flops | bytes accessed | tf_op | source)
XLA Modules:
  0.0 883.2 jit_solution(17926980350266696980)
XLA Ops:
  10.0 43.6 %all-gather = bf16[32,24,3]{1,2,0:T(4,128)(2,1)S(1)} all-gather(bf16[1,24,3]{1,2,0:T(4,128)(2,1)} %bitcast.217), channel_id=1, replica_groups=mesh['dp'=8,'fsdp'=4] {'dp','fsdp'}, dimensions={0}, use_global_device_ids=true | all-gather | bytes 4752 | tf_op jit(solution)/shard_map/all_gather | solution.py:54
  61.3 37.5 %all-reduce.21 = (bf16[768]{0:T(1024)(128)(2,1)S(1)}, bf16[768]{0:T(1024)(128)(2,1)S(1)}, bf16[768]{0:T(1024)(128)(2,1)S(1)}, bf16[768]{0:T(1024)(128)(2,1)S(1)}...) all-reduce(bf16[768]{0:T(1024)(128)(2,1)S(1)} %dynamic-update-slice, ...), channel_id=1, replica_groups=mesh['dp'=8,'fsdp'=4] {'dp','fsdp'}, use_global_device_ids=true, to_apply=%add.4 | all-reduce | flops 9216 | bytes 36864
  105.9 3.0 fusion.2
  112.2 17.9 %all-gather.8.cloned.1.call-done = bf16[768,768]{1,0:T(8,128)(2,1)} async-done(((bf16[24,768]{1,0:T(8,128)(2,1)}), bf16[768,768]{1,0:T(8,128)(2,1)}) %all-gather.8.cloned.1.call-update) | async-done | bytes 1179664 | tf_op jit(solution)/shard_map/all_gather | solution.py:44
  132.9 62.8 %all-gather.10.cloned.1.call-done = bf16[768,3072]{1,0:T(8,128)(2,1)} async-done(((bf16[24,3072]{1,0:T(8,128)(2,1)}), bf16[768,3072]{1,0:T(8,128)(2,1)}) %all-gather.10.cloned.1.call-update) | async-done | bytes 4718608 | tf_op jit(solution)/shard_map/all_gather | solution.py:50
  195.7 3.5 convolution_add_fusion.5
  199.2 61.7 %all-gather.12.cloned.1.call-done = bf16[3072,768]{1,0:T(8,128)(2,1)} async-done(((bf16[96,768]{1,0:T(8,128)(2,1)}), bf16[3072,768]{1,0:T(8,128)(2,1)}) %all-gather.12.cloned.1.call-update) | async-done | bytes 4718608 | tf_op jit(solution)/shard_map/all_gather | solution.py:52
  260.9 4.1 fusion.128
  281.5 2.3 copy.110
  287.2 2.6 fusion.132
  292.8 2.3 fusion.57
  298.1 5.5 convert_reduce_fusion.2
  303.6 2.3 multiply_reduce_fusion.5
  311.0 4.1 fusion.38
  323.2 2.0 multiply_reduce_fusion.8
  326.9 3.4 convert_reduce_fusion.1
  330.4 2.4 multiply_reduce_fusion.4
  350.7 2.0 multiply_reduce_fusion.7
  354.6 3.4 convert_reduce_fusion
  358.0 2.4 multiply_reduce_fusion.3
  365.4 3.8 add_add_fusion.3
  381.1 4.3 add_add_fusion.2
  386.4 2.9 fusion.108
  391.0 5.3 add_add_fusion.1
  397.2 3.8 fusion.109
  403.1 7.5 add_add_fusion
  411.9 4.1 fusion.112
  420.2 41.2 %all-reduce.20 = (f32[768]{0:T(1024)S(1)}, f32[768]{0:T(1024)S(1)}, f32[768]{0:T(1024)S(1)}, f32[768]{0:T(1024)S(1)}, f32[768]{0:T(1024)S(1)}, /*index=5*/f32[76...) all-reduce(f32[768]{0:T(1024)S(1)} %add_add_fusion.23, ...), channel_id=3, replica_groups=mesh['dp'=8,'fsdp'=4] {'dp','fsdp'}, use_global_device_ids=true, to_apply=%region_39.40.clone | all-reduce | flops 11520 | bytes 92160
  467.4 5.3 fusion.63
  472.7 119.9 %reduce-scatter.6.cloned.1.call-done = f32[24,2304]{1,0:T(8,128)} async-done(((f32[768,2304]{1,0:T(8,128)}), f32[24,2304]{1,0:T(8,128)}) %reduce-scatter.6.cloned.1.call-update) | async-done | bytes 221200 | tf_op jit(solution)/shard_map/reduce_scatter | solution.py:60
  592.5 141.2 %reduce-scatter.10.cloned.1.call-done = f32[24,3072]{1,0:T(8,128)} async-done(((f32[768,3072]{1,0:T(8,128)}), f32[24,3072]{1,0:T(8,128)}) %reduce-scatter.10.cloned.1.call-update) | async-done | bytes 294928 | tf_op jit(solution)/shard_map/reduce_scatter | solution.py:69
  733.7 142.1 %reduce-scatter.12.cloned.1.call-done = f32[96,768]{1,0:T(8,128)} async-done(((f32[3072,768]{1,0:T(8,128)}), f32[96,768]{1,0:T(8,128)}) %reduce-scatter.12.cloned.1.call-update) | async-done | bytes 294928 | tf_op jit(solution)/shard_map/reduce_scatter | solution.py:71
  (648 shorter events, 115.3 us)
Async XLA Ops:
  7.2 98.7 %all-gather.6.cloned.1.call-start = ((), (), s32[]{:S(2)}) async-start(), calls=%async_computation.4 | async-start | bytes 3649536 | tf_op jit(solution)/shard_map/all_gather | solution.py:41
  7.9 122.2 %all-gather.8.cloned.1.call-start = ((), (), s32[]{:S(2)}) async-start(), calls=%async_computation.5 | async-start | bytes 1216512 | tf_op jit(solution)/shard_map/all_gather | solution.py:44
  8.7 187.0 %all-gather.10.cloned.1.call-start = ((), (), s32[]{:S(2)}) async-start(), calls=%async_computation.6 | async-start | bytes 4866048 | tf_op jit(solution)/shard_map/all_gather | solution.py:50
  9.4 251.5 %all-gather.12.cloned.1.call-start = ((), (), s32[]{:S(2)}) async-start(), calls=%async_computation.7 | async-start | bytes 4866048 | tf_op jit(solution)/shard_map/all_gather | solution.py:52
  10.0 462.7 %reduce-scatter.8.cloned.1.call-start = ((), (), s32[]{:S(2)}) async-start(), calls=%async_computation.9 | async-start | bytes 2433024 | tf_op jit(solution)/shard_map/reduce_scatter | solution.py:63
  98.9 31.3 %copy-start.121 = (f32[768]{0:T(1024)}, f32[768]{0:T(1024)S(1)}, u32[]{:S(2)}) copy-start(f32[768]{0:T(1024)S(1)} %convert_element_type.269) | copy-start | bytes 9220
  103.5 26.6 %copy-start.117 = (f32[768]{0:T(1024)}, f32[768]{0:T(1024)S(1)}, u32[]{:S(2)}) copy-start(f32[768]{0:T(1024)S(1)} %get-tuple-element.77) | copy-start | bytes 9220
  111.7 18.5 %copy-start.15 = (bf16[192,768]{1,0:T(8,128)(2,1)S(1)}, bf16[192,768]{1,0:T(8,128)(2,1)}, u32[]{:S(2)}) copy-start(bf16[192,768]{1,0:T(8,128)(2,1)} %param.23) | copy-start | bytes 884740
  112.2 20.6 %copy-start.106 = (bf16[12,64,192]{2,1,0:T(8,128)(2,1)}, bf16[12,64,192]{2,1,0:T(8,128)(2,1)S(1)}, u32[]{:S(2)}) copy-start(bf16[12,64,192]{2,1,0:T(8,128)(2,1)S(1)} %convolution_convert_fusion) | copy-start | bytes 884740
  132.0 129.0 %copy-start.10 = (f32[192,768]{1,0:T(8,128)}, f32[192,768]{1,0:T(8,128)S(1)}, u32[]{:S(2)}) copy-start(f32[192,768]{1,0:T(8,128)S(1)} %get-tuple-element.132) | copy-start | bytes 1769476
  132.0 67.2 %copy-start.128 = (f32[192]{0:T(256)}, f32[192]{0:T(256)S(1)}, u32[]{:S(2)}) copy-start(f32[192]{0:T(256)S(1)} %broadcast_multiply_fusion.4) | copy-start | bytes 2308
  132.2 67.0 %copy-start.179 = (f32[192]{0:T(256)}, f32[192]{0:T(256)S(1)}, u32[]{:S(2)}) copy-start(f32[192]{0:T(256)S(1)} %multiply_reduce_fusion.19) | copy-start | bytes 2308
  132.2 67.0 %copy-start.139 = (f32[192]{0:T(256)}, f32[192]{0:T(256)S(1)}, u32[]{:S(2)}) copy-start(f32[192]{0:T(256)S(1)} %fusion.84) | copy-start | bytes 2308
  199.2 67.1 %copy-start.27 = (f32[192,3072]{1,0:T(8,128)}, f32[192,3072]{1,0:T(8,128)S(1)}, u32[]{:S(2)}) copy-start(f32[192,3072]{1,0:T(8,128)S(1)} %convolution_add_fusion.5) | copy-start | bytes 7077892
  265.0 7.7 copy-start.21
  274.0 58.7 %copy-start.8 = (f32[192,768]{1,0:T(8,128)}, f32[192,768]{1,0:T(8,128)S(1)}, u32[]{:S(2)}) copy-start(f32[192,768]{1,0:T(8,128)S(1)} %get-tuple-element.138) | copy-start | bytes 1769476
  277.7 17.5 %copy-start.24 = (f32[192,768]{1,0:T(8,128)}, f32[192,768]{1,0:T(8,128)S(1)}, u32[]{:S(2)}) copy-start(f32[192,768]{1,0:T(8,128)S(1)} %get-tuple-element.140) | copy-start | bytes 1769476
  289.9 6.2 slice-start.12
  295.8 10.2 %copy-start.17 = (f32[192,768]{1,0:T(8,128)}, f32[192,768]{1,0:T(8,128)S(1)}, u32[]{:S(2)}) copy-start(f32[192,768]{1,0:T(8,128)S(1)} %get-tuple-element.144) | copy-start | bytes 1769476
  295.8 10.2 %copy-start.134 = (f32[192]{0:T(256)}, f32[192]{0:T(256)S(1)}, u32[]{:S(2)}) copy-start(f32[192]{0:T(256)S(1)} %broadcast_multiply_fusion) | copy-start | bytes 2308
  296.3 9.7 %copy-start.148 = (f32[192]{0:T(256)}, f32[192]{0:T(256)S(1)}, u32[]{:S(2)}) copy-start(f32[192]{0:T(256)S(1)} %fusion.88) | copy-start | bytes 2308
  307.9 7.3 slice-start
  315.4 6.4 copy-start.33
  326.4 6.6 copy-start.19
  339.7 7.2 copy-start.35
  344.2 6.4 copy-start.66
  353.9 6.8 copy-start.29
  369.3 223.3 %reduce-scatter.6.cloned.1.call-start = ((), (), s32[]{:S(2)}) async-start(), calls=%async_computation.8 | async-start | bytes 7299072 | tf_op jit(solution)/shard_map/reduce_scatter | solution.py:60
  374.2 6.7 copy-start.82
  385.4 348.4 %reduce-scatter.10.cloned.1.call-start = ((), (), s32[]{:S(2)}) async-start(), calls=%async_computation.10 | async-start | bytes 9732096 | tf_op jit(solution)/shard_map/reduce_scatter | solution.py:69
  396.3 479.6 %reduce-scatter.12.cloned.1.call-start = ((), (), s32[]{:S(2)}) async-start(), calls=%async_computation.11 | async-start | bytes 9732096 | tf_op jit(solution)/shard_map/reduce_scatter | solution.py:71
  416.5 50.8 %copy-start.188 = (f32[768]{0:T(1024)S(1)}, f32[768]{0:T(1024)}, u32[]{:S(2)}) copy-start(f32[768]{0:T(1024)} %convert_element_type.275) | copy-start | bytes 9220
  (199 other events, 479.9 us)
Sparse Core Ops, SparseCore 0:
  10.9 63.4 all-gather.5
  77.3 52.8 all-gather.7
  133.1 62.5 all-gather.9
  198.4 62.4 all-gather.11
  369.4 97.8 reduce-scatter.7
  474.3 118.1 reduce-scatter.5
  599.0 134.6 reduce-scatter.9
  741.2 134.6 reduce-scatter.11
where the time goes:
time: 887 us; the launch traced here: 883 us
  waiting for transfers between devices  548 us (62%)
  blocking collectives  122 us (14%)
  matrix products  120 us (14%)
  local copies, waits for them, and re-layouts  46.6 us (5%)
  other arithmetic  27.7 us (3%)
  between operations  17.6 us (2%)
    reduce_scatter x1, waiting for transfers between devices, reduce_total(): lax.psum_scatter(grad_set[11], ('dp', 'fsdp'), scatter_dimension=0, tiled...  142 us
    reduce_scatter x1, waiting for transfers between devices, reduce_total(): lax.psum_scatter(grad_set[9], ('dp', 'fsdp'), scatter_dimension=0, tiled=...  141 us
    reduce_scatter x1, waiting for transfers between devices, reduce_total(): lax.psum_scatter(grad_set[0], ('dp', 'fsdp'), scatter_dimension=0, tiled=...  120 us
    unnamed x2, blocking collectives  78.8 us
    all_gather x1, waiting for transfers between devices, fetch_once(): lax.all_gather(w_up, ('dp', 'fsdp'), axis=0, tiled=True)  62.8 us
    all_gather x1, waiting for transfers between devices, fetch_once(): lax.all_gather(w_down, ('dp', 'fsdp'), axis=0, tiled=True)  61.7 us
    all_gather x1, blocking collectives, fetch_once(): lax.all_gather(pass_embed, ('dp', 'fsdp'), axis=1, tiled=True)  43.6 us
    unnamed x475, local copies, waits for them, and re-layouts  30.3 us
  transfers between devices with their start and end apart: 8, of which 6 were waited for; matrix products, arithmetic and copies ran while one was open for 9% of the time, Pallas kernels for 0%

commit v1 on v0

--- a/solution.py
+++ b/solution.py
@@ -1,77 +1,272 @@
+import functools
+
 import jax
 import jax.numpy as jnp
 from jax import lax
+from jax.experimental import pallas as pl
+from jax.experimental.pallas import tpu as pltpu
 from jax.sharding import PartitionSpec as P
 
 HEAD_DIM = 64
 PASSES = 3
-
-
 EPSILON = 1e-05
+AXES = ("dp", "fsdp")
+F32 = jnp.float32
+BF16 = jnp.bfloat16
+
+
+def pairs(partner):
+    return [(i, partner(i)) for i in range(32)]
+
+
+TO_MATE = pairs(lambda i: i ^ 1)
+TO_Z = [pairs(lambda i, k=k: i ^ (8 * k)) for k in range(4)]
+TO_NEAR = pairs(lambda i: i ^ (2 if i & 1 else 4))
+TO_FAR = pairs(lambda i: i ^ (4 if i & 1 else 2))
+
+
+def send(x, route):
+    return lax.ppermute(x, AXES, route)
+
+
+def after(x, *earlier):
+    earlier = tuple(e for e in earlier if e is not None)
+    return lax.optimization_barrier((x, earlier))[0] if earlier else x
+
+
+def in_core_order(core, mine, other, axis):
+    return jnp.where(
+        core == 0,
+        jnp.concatenate([mine, other], axis=axis),
+        jnp.concatenate([other, mine], axis=axis),
+    )
+
+
+def gather_chunks(blocks):
+    pieces, crossed, far = [], [], []
+    for n, block in enumerate(blocks):
+        if n >= 1:
+            block = after(block, crossed[n - 1])
+        z = [send(block, TO_Z[k]) for k in (1, 2, 3)]
+        crossed.append(z)
+        stack = jnp.stack([block] + z)
+        if n >= 2:
+            stack = after(stack, far[n - 2])
+        both = jnp.stack([stack, send(stack, TO_NEAR)])
+        distant = send(both, TO_FAR)
+        far.append(distant)
+        pieces.append([both, distant, send(both, TO_MATE), send(distant, TO_MATE)])
+    return pieces
+
+
+def chip_of(place, swapped, far, near, z):
+    chip, core = place
+    order = core ^ swapped
+    near_bit = 2 - order
+    far_bit = 1 + order
+    return chip ^ (far * far_bit) ^ (near * near_bit) ^ (z * 4)
+
+
+def run_copies(copies):
+    for copy in copies:
+        copy.start()
+    for copy in copies:
+        copy.wait()
+
+
+def assemble_kernel(widths, place_ref, both, distant, mate_both, mate_distant, *rest):
+    outs, sem = rest[:-1], rest[-1]
+    place = (place_ref[0], place_ref[1])
+    rows = both.shape[2]
+    copies = []
+    for source, swapped, far in (
+        (both, 0, 0),
+        (distant, 0, 1),
+        (mate_both, 1, 0),
+        (mate_distant, 1, 1),
+    ):
+        half = place[1] ^ swapped
+        for near in range(2):
+            for z in range(4):
+                chip = chip_of(place, swapped, far, near, z)
+                first = 0
+                for out, width in zip(outs, widths):
+                    copies.append(
+                        pltpu.make_async_copy(
+                            source.at[near, z, :, pl.ds(first, width)],
+                            out.at[
+                                pl.ds(pl.multiple_of(chip * rows, 16), rows),
+                                pl.ds(pl.multiple_of(half * width, 128), width),
+                            ],
+                            sem,
+                        )
+                    )
+                    first += width
+    run_copies(copies)
+
+
+def assemble(place, pieces, widths):
+    rows = pieces[0].shape[2] * 16
+    anywhere = pl.BlockSpec(memory_space=pl.ANY)
+    return pl.pallas_call(
+        functools.partial(assemble_kernel, widths),
+        out_shape=[jax.ShapeDtypeStruct((rows, 2 * w), BF16) for w in widths],
+        in_specs=[pl.BlockSpec(memory_space=pltpu.SMEM)] + [anywhere] * 4,
+        out_specs=[anywhere] * len(widths),
+        scratch_shapes=[pltpu.SemaphoreType.DMA(())],
+    )(place, *pieces)
+
+
+def spread_kernel(widths, place_ref, *refs):
+    count = len(widths)
+    sources, (give, keep), sem = refs[:count], refs[count : count + 2], refs[-1]
+    place = (place_ref[0], place_ref[1])
+    rows = give.shape[3]
+    copies = []
+    for target, swapped in ((give, 1), (keep, 0)):
+        half = place[1] ^ swapped
+        for far in range(2):
+            for near in range(2):
+                for z in range(4):
+                    chip = chip_of(place, swapped, far, near, z)
+                    first = 0
+                    for source, width in zip(sources, widths):
+                        copies.append(
+                            pltpu.make_async_copy(
+                                source.at[
+                                    pl.ds(pl.multiple_of(chip * rows, 16), rows),
+                                    pl.ds(pl.multiple_of(half * width, 128), width),
+                                ],
+                                target.at[far, near, z, :, pl.ds(first, width)],
+                                sem,
+                            )
+                        )
+                        first += width
+    run_copies(copies)
+
+
+def spread(place, grads):
+    widths = [g.shape[1] // 2 for g in grads]
+    rows = grads[0].shape[0] // 16
+    anywhere = pl.BlockSpec(memory_space=pl.ANY)
+    shape = jax.ShapeDtypeStruct((2, 2, 4, rows, sum(widths)), BF16)
+    return pl.pallas_call(
+        functools.partial(spread_kernel, widths),
+        out_shape=[shape, shape],
+        in_specs=[pl.BlockSpec(memory_space=pltpu.SMEM)] + [anywhere] * len(grads),
+        out_specs=[anywhere] * 2,
+        scratch_shapes=[pltpu.SemaphoreType.DMA(())],
+    )(place, *grads)
+
+
+def add_low(a, b):
+    return (a.astype(F32) + b.astype(F32)).astype(BF16)
+
+
+def scatter_chunk(core, give, keep, earlier):
+    got = send(give, TO_MATE)
+    give, keep = add_low(keep[1], got[1]), add_low(keep[0], got[0])
+    got = send(after(give, earlier.get("near")), TO_FAR)
+    give, keep = add_low(keep[1], got[1]), add_low(keep[0], got[0])
+    got = send(give, TO_NEAR)
+    near = got
+    give = [add_low(keep[k], got[k]) for k in (1, 2, 3)]
+    total = keep[0].astype(F32) + got[0].astype(F32)
+    give = after(give, earlier.get("z"))
+    z = [send(give[k - 1], TO_Z[k]) for k in (1, 2, 3)]
+    for part in z:
+        total = total + part.astype(F32)
+    rows = total.shape[0] // 2
+    total = total.reshape(2, rows, total.shape[1])
+    mine = jnp.where(core == 0, total[0], total[1])
+    other = send(jnp.where(core == 0, total[1], total[0]), TO_MATE)
+    return (
+        jnp.where(core == 0, mine, other),
+        jnp.where(core == 0, other, mine),
+    ), {"near": near, "z": z}
+
+
+SMALL = 256
+
+
+def pack_small(vectors, bias_up, pass_embed):
+    rows = vectors[0].shape[0]
+    first = jnp.stack(vectors, axis=1)
+    second = jnp.concatenate([bias_up.reshape(rows, -1), pass_embed.T], axis=1)
+    pad = lambda a: jnp.pad(a, ((0, 0), (0, SMALL // 2 - a.shape[1])))
+    return jnp.concatenate([pad(first), pad(second)], axis=1)
+
+
+def unpack_small(small):
+    half = SMALL // 2
+    vectors = [small[:, k] for k in range(8)]
+    return vectors, small[:, half : half + 4].reshape(-1), small[:, half + 4 : half + 4 + PASSES].T
+
+
+def is_known_slice():
+    return lax.axis_size("dp") == 8 and lax.axis_size("fsdp") == 4
+
+
+def place_of():
+    index = lax.axis_index("dp") * 4 + lax.axis_index("fsdp")
+    return jnp.stack([index >> 1, index & 1]).astype(jnp.int32)
+
+
+def halves(*arrays):
+    return [
+        jnp.concatenate([a[:, h * (a.shape[1] // 2) : (h + 1) * (a.shape[1] // 2)] for a in arrays], axis=1)
+        for h in range(2)
+    ]
+
+
+def gather_all(w_qkv, w_out, small, w_up, w_down):
+    if not is_known_slice():
+        return [lax.all_gather(a, AXES, axis=0, tiled=True) for a in (w_qkv, w_out, small, w_up, w_down)]
+    place = place_of()
+    core = place[1]
+    blocks = []
+    for arrays in ((w_qkv, w_out, small), (w_up,), (w_down,)):
+        low, high = halves(*arrays)
+        mine = jnp.where(core == 0, low, high)
+        other = send(jnp.where(core == 0, high, low), TO_MATE)
+        blocks.append(in_core_order(core, mine, other, 0))
+    pieces = gather_chunks(blocks)
+    full = assemble(place, pieces[0], [a.shape[1] // 2 for a in (w_qkv, w_out, small)])
+    full += assemble(place, pieces[1], [w_up.shape[1] // 2])
+    full += assemble(place, pieces[2], [w_down.shape[1] // 2])
+    return full
+
+
+def scatter_all(chunks):
+    if not is_known_slice():
+        return [
+            [lax.psum_scatter(g.astype(F32), AXES, scatter_dimension=0, tiled=True) for g in grads]
+            for grads in chunks
+        ]
+    place = place_of()
+    core = place[1]
+    results, earlier = [], {}
+    for grads in chunks:
+        give, keep = spread(place, grads)
+        (low, high), earlier = scatter_chunk(core, give, keep, earlier)
+        first, out = 0, []
+        for g in grads:
+            width = g.shape[1] // 2
+            out.append(jnp.concatenate([low[:, first : first + width], high[:, first : first + width]], axis=1))
+            first += width
+        results.append(out)
+    return results
 
 
 def layer_norm(values, gain_vec, shift_vec):
     average = jnp.mean(values, axis=-1, keepdims=True)
     centred = values - average
-    spread = jnp.mean(centred * centred, axis=-1, keepdims=True)
-    return centred * lax.rsqrt(spread + EPSILON) * gain_vec + shift_vec
+    spread_ = jnp.mean(centred * centred, axis=-1, keepdims=True)
+    return centred * lax.rsqrt(spread_ + EPSILON) * gain_vec + shift_vec
 
 
 def gelu_tanh(values):
     return jax.nn.gelu(values, approximate=True)
-
-
-def fetch_once(
-    w_qkv,
-    bias_q,
-    bias_v,
-    w_out,
-    bias_out,
-    gain_attn,
-    shift_attn,
-    gain_mlp,
-    shift_mlp,
-    w_up,
-    bias_up,
-    w_down,
-    bias_down,
-    pass_embed,
-):
-    return (
-        lax.all_gather(w_qkv, ("dp", "fsdp"), axis=0, tiled=True),
-        lax.all_gather(bias_q, ("dp", "fsdp"), axis=0, tiled=True),
-        lax.all_gather(bias_v, ("dp", "fsdp"), axis=0, tiled=True),
-        lax.all_gather(w_out, ("dp", "fsdp"), axis=0, tiled=True),
-        lax.all_gather(bias_out, ("dp", "fsdp"), axis=0, tiled=True),
-        lax.all_gather(gain_attn, ("dp", "fsdp"), axis=0, tiled=True),
-        lax.all_gather(shift_attn, ("dp", "fsdp"), axis=0, tiled=True),
-        lax.all_gather(gain_mlp, ("dp", "fsdp"), axis=0, tiled=True),
-        lax.all_gather(shift_mlp, ("dp", "fsdp"), axis=0, tiled=True),
-        lax.all_gather(w_up, ("dp", "fsdp"), axis=0, tiled=True),
-        lax.all_gather(bias_up, ("dp", "fsdp"), axis=0, tiled=True),
-        lax.all_gather(w_down, ("dp", "fsdp"), axis=0, tiled=True),
-        lax.all_gather(bias_down, ("dp", "fsdp"), axis=0, tiled=True),
-        lax.all_gather(pass_embed, ("dp", "fsdp"), axis=1, tiled=True),
-    )
-
-
-def reduce_total(grad_set):
-    return (
-        lax.psum_scatter(grad_set[0], ("dp", "fsdp"), scatter_dimension=0, tiled=True),
-        lax.psum_scatter(grad_set[1], ("dp", "fsdp"), scatter_dimension=0, tiled=True),
-        lax.psum_scatter(grad_set[2], ("dp", "fsdp"), scatter_dimension=0, tiled=True),
-        lax.psum_scatter(grad_set[3], ("dp", "fsdp"), scatter_dimension=0, tiled=True),
-        lax.psum_scatter(grad_set[4], ("dp", "fsdp"), scatter_dimension=0, tiled=True),
-        lax.psum_scatter(grad_set[5], ("dp", "fsdp"), scatter_dimension=0, tiled=True),
-        lax.psum_scatter(grad_set[6], ("dp", "fsdp"), scatter_dimension=0, tiled=True),
-        lax.psum_scatter(grad_set[7], ("dp", "fsdp"), scatter_dimension=0, tiled=True),
-        lax.psum_scatter(grad_set[8], ("dp", "fsdp"), scatter_dimension=0, tiled=True),
-        lax.psum_scatter(grad_set[9], ("dp", "fsdp"), scatter_dimension=0, tiled=True),
-        lax.psum_scatter(grad_set[10], ("dp", "fsdp"), scatter_dimension=0, tiled=True),
-        lax.psum_scatter(grad_set[11], ("dp", "fsdp"), scatter_dimension=0, tiled=True),
-        lax.psum_scatter(grad_set[12], ("dp", "fsdp"), scatter_dimension=0, tiled=True),
-        lax.psum_scatter(grad_set[13], ("dp", "fsdp"), scatter_dimension=1, tiled=True),
-    )
 
 
 def masked_scores(queries, key_stack, allowed):
@@ -322,10 +517,19 @@
 ):
     length, model_width = tokens.shape
     position = jnp.arange(length, dtype=jnp.int32)
-    doc_ends = jnp.cumsum(lengths[0])
+    docs = lengths.shape[1]
+    upto = jnp.arange(docs)[:, None] <= jnp.arange(docs)[None, :]
+    doc_ends = jnp.sum(jnp.where(upto, lengths[0][:, None], 0), axis=0)
     doc_ids = jnp.sum((position[:, None] >= doc_ends[None, :]).astype(jnp.int32), axis=1)
     allowed_base = (doc_ids[:, None] == doc_ids[None, :]) & (position[None, :] <= position[:, None])
-    gathered = fetch_once(
+    small = pack_small(
+        [bias_q, bias_v, bias_out, gain_attn, shift_attn, gain_mlp, shift_mlp, bias_down], bias_up, pass_embed
+    )
+    w_qkv, w_out, small, w_up, w_down = gather_all(w_qkv, w_out, small, w_up, w_down)
+    (bias_q, bias_v, bias_out, gain_attn, shift_attn, gain_mlp, shift_mlp, bias_down), bias_up, pass_embed = unpack_small(
+        small
+    )
+    gathered = (
         w_qkv,
         bias_q,
         bias_v,
@@ -372,24 +576,29 @@
             if totals is None
             else tuple((running + extra for running, extra in zip(totals, pass_grads)))
         )
-    totals = reduce_total(totals)
+    (g_qkv, g_bq, g_bv, g_out, g_bo, g_ga, g_sa, g_gm, g_sm, g_up, g_bu, g_down, g_bd, g_pe) = totals
+    g_small = pack_small([g_bq, g_bv, g_bo, g_ga, g_sa, g_gm, g_sm, g_bd], g_bu, g_pe)
+    (g_down,), (g_up,), (g_qkv, g_out, g_small) = scatter_all(
+        [[g_down.astype(BF16)], [g_up.astype(BF16)], [g_qkv.astype(BF16), g_out.astype(BF16), g_small.astype(BF16)]]
+    )
+    (g_bq, g_bv, g_bo, g_ga, g_sa, g_gm, g_sm, g_bd), g_bu, g_pe = unpack_small(g_small)
     return (
         output,
         grad_state.astype(jnp.bfloat16),
-        totals[0],
-        totals[1],
-        totals[2],
-        totals[3],
-        totals[4],
-        totals[5],
-        totals[6],
-        totals[7],
-        totals[8],
-        totals[9],
-        totals[10],
-        totals[11],
-        totals[12],
-        totals[13],
+        g_qkv,
+        g_bq,
+        g_bv,
+        g_out,
+        g_bo,
+        g_ga,
+        g_sa,
+        g_gm,
+        g_sm,
+        g_up,
+        g_bu,
+        g_down,
+        g_bd,
+        g_pe,
     )
 
 

time: 887 us -> 1290 us (1.45)
  Pallas kernels: 0 us -> 892 us
  waiting for transfers between devices: 548 us -> 117 us
  blocking collectives: 122 us -> 0 us
  starting transfers between devices: 0.78 us -> 50.1 us
  other arithmetic: 27.7 us -> 50.8 us
  between operations: 17.6 us -> 4.15 us
    pallas_call x0 -> x6, Pallas kernels: none -> 892 us  [the longest x3 446 us: spread(): pl.pallas_call(functools.partial(spread_kernel, widths), out_shape=[shape...]
    reduce_scatter x4 -> x0, waiting for transfers between devices: 403 us -> none  [the longest x1 142 us: reduce_total(): lax.psum_scatter(grad_set[11], ('dp', 'fsdp'), scatter_dimension=0, tiled...]
    all_gather x4 -> x0, waiting for transfers between devices: 142 us -> none  [the longest x1 62.8 us: fetch_once(): lax.all_gather(w_up, ('dp', 'fsdp'), axis=0, tiled=True)]
    ppermute x0 -> x45, waiting for transfers between devices: none -> 117 us  [send(): return lax.ppermute(x, AXES, route)]
    unnamed x2 -> x0, blocking collectives: 78.8 us -> none
    ppermute x0 -> x45, starting transfers between devices: none -> 50.1 us  [send(): return lax.ppermute(x, AXES, route)]
    all_gather x1 -> x0, blocking collectives: 43.6 us -> none  [fetch_once(): lax.all_gather(pass_embed, ('dp', 'fsdp'), axis=1, tiled=True)]
    unnamed x475 -> x496, local copies, waits for them, and re-layouts: 30.3 us -> 15.4 us
  transfers between devices with their start and end apart: 8 -> 45, of which waited for: 6 -> 19; matrix products, arithmetic and copies ran while one was open for 9% -> 5% of each run, Pallas kernels for 0% -> 47%
where the time goes in v1:
time: 1290 us; the launch traced here: 1280 us
  Pallas kernels  892 us (69%)
  matrix products  122 us (9%)
  waiting for transfers between devices  117 us (9%)
  other arithmetic  50.8 us (4%)
  starting transfers between devices  50.1 us (4%)
  local copies, waits for them, and re-layouts  48.2 us (4%)
    pallas_call x3, Pallas kernels, spread(): pl.pallas_call(functools.partial(spread_kernel, widths), out_shape=[shape...  446 us
    pallas_call x3, Pallas kernels, assemble(): pl.pallas_call(functools.partial(assemble_kernel, widths), out_shape=[jax...  446 us
    ppermute x45, waiting for transfers between devices, send(): return lax.ppermute(x, AXES, route)  117 us
    ppermute x45, starting transfers between devices, send(): return lax.ppermute(x, AXES, route)  50.1 us
  transfers between devices with their start and end apart: 45, of which 19 were waited for; matrix products, arithmetic and copies ran while one was open for 5% of the time, Pallas kernels for 47%

profile of v1, /device:TPU:0, one launch (start us, length us, event | category | flops | bytes accessed | tf_op | source)
XLA Modules:
  0.0 1284.1 jit_solution(585950893360736741)
XLA Ops:
  7.6 4.8 collective-permute-start.3
  13.1 4.4 collective-permute-done.3
  17.5 9.0 collective-permute-done.2
  34.1 6.5 collective-permute-done.10
  44.0 13.0 %collective-permute-done.12 = bf16[4,48,1536]{2,1,0:T(8,128)(2,1)S(1)} collective-permute-done((bf16[4,48,1536]{2,1,0:T(8,128)(2,1)S(1)}, bf16[4,48,1536]{2,1,0:T(8,128)(2,1)S(1)}, u32[]{:S(2)}, u32[]{:S(2)}) %collective-permute-start.12) | collective-permute-done | bytes 589856 | tf_op jit(solution)/shard_map/ppermute | solution.py:29
  63.0 10.6 collective-permute-done.13.distant
  74.7 4.6 collective-permute-start.18
  79.4 7.2 collective-permute-done.18
  86.5 5.2 collective-permute-done.17
  96.1 5.8 collective-permute-done.20
  105.1 144.7 %shard_map.289 = bf16[768,3072]{1,0:T(8,128)(2,1)} custom-call(s32[2]{0:T(128)} %pad_add_fusion.place_ref, bf16[2,4,48,1536]{3,2,1,0:T(8,128)(2,1)} %copy-done.50, bf16[2,4,48,1536]{3,2,1,0:T(8,128)(2,1)} %collective-permute-done.13.distant, bf16[2,4,48,1536]{3,2,1,0:T(8,128)(2,1)} %collective-permute-done.14.mate_both, ...), custom_call_target="tpu_custom_call" | custom-call | tf_op jit(solution)/shard_map/pallas_call | solution.py:111
  249.9 156.7 %shard_map.288 = (bf16[768,2304]{1,0:T(8,128)(2,1)}, bf16[768,768]{1,0:T(8,128)(2,1)}, bf16[768,256]{1,0:T(8,128)(2,1)}) custom-call(s32[2]{0:T(128)} %pad_add_fusion.place_ref, bf16[2,4,48,1664]{3,2,1,0:T(8,128)(2,1)} %copy-done.49, bf16[2,4,48,1664]{3,2,1,0:T(8,128)(2,1)} %collective-permute-done.5.distant, ...), custom_call_target="tpu_custom_call" | custom-call | tf_op jit(solution)/shard_map/pallas_call | solution.py:111
  422.9 144.7 %shard_map.290 = bf16[3072,768]{1,0:T(8,128)(2,1)} custom-call(s32[2]{0:T(128)} %pad_add_fusion.place_ref, bf16[2,4,192,384]{3,2,1,0:T(8,128)(2,1)} %pad_maximum_fusion.2.both, bf16[2,4,192,384]{3,2,1,0:T(8,128)(2,1)} %collective-permute-done.21.distant, bf16[2,4,192,384]{3,2,1,0:T(8,128)(2,1)} %collective-permute-done.22.mate_both, ...), custom_call_target="tpu_custom_call" | custom-call | tf_op jit(solution)/shard_map/pallas_call | solution.py:111
  567.6 5.0 fusion.180
  619.8 4.1 fusion.38
  661.7 3.4 convert_reduce_fusion
  682.2 5.2 fusion.157
  687.4 5.1 fusion.156
  692.6 5.7 fusion.160
  698.3 5.5 fusion.149
  712.9 10.5 add_convert_fusion.1.refs_0_
  723.4 144.8 %shard_map.292 = (bf16[2,2,4,48,1536]{4,3,2,1,0:T(8,128)(2,1)}, bf16[2,2,4,48,1536]{4,3,2,1,0:T(8,128)(2,1)}) custom-call(s32[2]{0:T(128)} %pad_add_fusion.place_ref, bf16[768,3072]{1,0:T(8,128)(2,1)} %add_convert_fusion.1.refs_0_), custom_call_target="tpu_custom_call" | custom-call | tf_op jit(solution)/shard_map/pallas_call | solution.py:153
  868.4 10.1 add_convert_fusion.refs_0_
  878.7 144.9 %shard_map.293 = (bf16[2,2,4,192,384]{4,3,2,1,0:T(8,128)(2,1)}, bf16[2,2,4,192,384]{4,3,2,1,0:T(8,128)(2,1)}) custom-call(s32[2]{0:T(128)} %pad_add_fusion.place_ref, bf16[3072,768]{1,0:T(8,128)(2,1)} %add_convert_fusion.refs_0_), custom_call_target="tpu_custom_call" | custom-call | tf_op jit(solution)/shard_map/pallas_call | solution.py:153
  1035.2 3.4 add_convert_fusion.6
  1044.3 156.7 %shard_map.291 = (bf16[2,2,4,48,1664]{4,3,2,1,0:T(8,128)(2,1)}, bf16[2,2,4,48,1664]{4,3,2,1,0:T(8,128)(2,1)}) custom-call(s32[2]{0:T(128)} %pad_add_fusion.place_ref, bf16[768,2304]{1,0:T(8,128)(2,1)} %add_convert_fusion.2.refs_0_, bf16[768,768]{1,0:T(8,128)(2,1)} %add_convert_fusion.9.refs_1_, bf16[768,256]{1,0:T(8,128)(2,1)} %fusion.89.refs_2_), custom_call_target="tpu_custom_call" | custom-call | tf_op jit(solution)/shard_map/pallas_call | solution.py:153
  1205.5 6.1 collective-permute-done.28
  1217.2 10.6 collective-permute-done.29
  1230.2 7.8 collective-permute-done.30
  1246.6 8.9 collective-permute-done.31
  1257.1 9.2 collective-permute-done.32
  1274.0 4.8 collective-permute-done.40
  (798 shorter events, 211.0 us)
Async XLA Ops:
  12.4 14.1 %collective-permute-start.2 = (bf16[48,1664]{1,0:T(8,128)(2,1)S(1)}, bf16[48,1664]{1,0:T(8,128)(2,1)S(1)}, u32[]{:S(2)}, u32[]{:S(2)}) collective-permute-start(bf16[48,1664]{1,0:T(8,128)(2,1)S(1)} %maximum_select_fusion.1), channel_id=1, source_target_pairs={{0,16},{1,17},{2,18},{3,19},{4,20},{5,21},{6,22},{7,23},{8,24},{9,... | collective-permute-start | bytes 479240 | tf_op jit(solution)/shard_map/ppermute | solution.py:29
  12.4 14.1 %collective-permute-start.1 = (bf16[48,1664]{1,0:T(8,128)(2,1)S(1)}, bf16[48,1664]{1,0:T(8,128)(2,1)S(1)}, u32[]{:S(2)}, u32[]{:S(2)}) collective-permute-start(bf16[48,1664]{1,0:T(8,128)(2,1)S(1)} %maximum_select_fusion.1), channel_id=1, source_target_pairs={{0,8},{1,9},{2,10},{3,11},{4,12},{5,13},{6,14},{7,15},{8,0},{9,1},... | collective-permute-start | bytes 479240 | tf_op jit(solution)/shard_map/ppermute | solution.py:29
  26.5 14.1 %collective-permute-start.10 = (bf16[48,1536]{1,0:T(8,128)(2,1)S(1)}, bf16[48,1536]{1,0:T(8,128)(2,1)S(1)}, u32[]{:S(2)}, u32[]{:S(2)}) collective-permute-start(bf16[48,1536]{1,0:T(8,128)(2,1)S(1)} %maximum_select_fusion.2), channel_id=1, source_target_pairs={{0,16},{1,17},{2,18},{3,19},{4,20},{5,21},{6,22},{7,23},{8,24},{9,... | collective-permute-start | bytes 442376 | tf_op jit(solution)/shard_map/ppermute | solution.py:29
  29.5 11.1 collective-permute-start.11
  31.0 11.3 collective-permute-start.4
  40.7 16.3 %collective-permute-start.12 = (bf16[4,48,1536]{2,1,0:T(8,128)(2,1)S(1)}, bf16[4,48,1536]{2,1,0:T(8,128)(2,1)S(1)}, u32[]{:S(2)}, u32[]{:S(2)}) collective-permute-start(bf16[4,48,1536]{2,1,0:T(8,128)(2,1)S(1)} %get-tuple-element.251), channel_id=1, source_target_pairs={{0,4},{1,3},{2,6},{3,1},{4,0},{5,7},{6,2},{7,5},{8,12},{9,11},{10,... | collective-permute-start | bytes 1769480 | tf_op jit(solution)/shard_map/ppermute | solution.py:29
  42.5 20.0 %collective-permute-start.5 = (bf16[2,4,48,1664]{3,2,1,0:T(8,128)(2,1)S(1)}, bf16[2,4,48,1664]{3,2,1,0:T(8,128)(2,1)}, u32[]{:S(2)}, u32[]{:S(2)}) collective-permute-start(bf16[2,4,48,1664]{3,2,1,0:T(8,128)(2,1)S(1)} %pad_maximum_fusion.both), channel_id=1, source_target_pairs={{0,2},{1,5},{2,0},{3,7},{4,6},{5,1},{6,4},{7,3},{8,10},{9,13},{10,... | collective-permute-start | bytes 3833864 | tf_op jit(solution)/shard_map/ppermute | solution.py:29
  57.2 16.4 %collective-permute-start.13 = (bf16[2,4,48,1536]{3,2,1,0:T(8,128)(2,1)S(1)}, bf16[2,4,48,1536]{3,2,1,0:T(8,128)(2,1)}, u32[]{:S(2)}, u32[]{:S(2)}) collective-permute-start(bf16[2,4,48,1536]{3,2,1,0:T(8,128)(2,1)S(1)} %pad_maximum_fusion.1.both), channel_id=1, source_target_pairs={{0,2},{1,5},{2,0},{3,7},{4,6},{5,1},{6,4},{7,3},{8,10},{9,13},{10,... | collective-permute-start | bytes 3538952 | tf_op jit(solution)/shard_map/ppermute | solution.py:29
  60.1 14.6 %collective-permute-start.19 = (bf16[192,384]{1,0:T(8,128)(2,1)S(1)}, bf16[192,384]{1,0:T(8,128)(2,1)S(1)}, u32[]{:S(2)}, u32[]{:S(2)}) collective-permute-start(bf16[192,384]{1,0:T(8,128)(2,1)S(1)} %maximum_select_fusion.3), channel_id=1, source_target_pairs={{0,24},{1,25},{2,26},{3,27},{4,28},{5,29},{6,30},{7,31},{8,16},{9,... | collective-permute-start | bytes 442376 | tf_op jit(solution)/shard_map/ppermute | solution.py:29
  62.4 187.4 %collective-permute-start.6 = (bf16[2,4,48,1664]{3,2,1,0:T(8,128)(2,1)S(1)}, bf16[2,4,48,1664]{3,2,1,0:T(8,128)(2,1)}, u32[]{:S(2)}, u32[]{:S(2)}) collective-permute-start(bf16[2,4,48,1664]{3,2,1,0:T(8,128)(2,1)S(1)} %pad_maximum_fusion.both), channel_id=1, source_target_pairs={{0,1},{1,0},{2,3},{3,2},{4,5},{5,4},{6,7},{7,6},{8,9},{9,8},{10,11... | collective-permute-start | bytes 3833864 | tf_op jit(solution)/shard_map/ppermute | solution.py:29
  62.5 187.4 %collective-permute-start.7 = (bf16[2,4,48,1664]{3,2,1,0:T(8,128)(2,1)}, bf16[2,4,48,1664]{3,2,1,0:T(8,128)(2,1)}, u32[]{:S(2)}, u32[]{:S(2)}) collective-permute-start(bf16[2,4,48,1664]{3,2,1,0:T(8,128)(2,1)} %collective-permute-done.5.distant), channel_id=1, source_target_pairs={{0,1},{1,0},{2,3},{3,2},{4,5},{5,4},{6,7},{7,6},{8,9},{9,8},{10,11... | collective-permute-start | bytes 3833864 | tf_op jit(solution)/shard_map/ppermute | solution.py:29
  63.0 42.2 %collective-permute-start.14 = (bf16[2,4,48,1536]{3,2,1,0:T(8,128)(2,1)S(1)}, bf16[2,4,48,1536]{3,2,1,0:T(8,128)(2,1)}, u32[]{:S(2)}, u32[]{:S(2)}) collective-permute-start(bf16[2,4,48,1536]{3,2,1,0:T(8,128)(2,1)S(1)} %pad_maximum_fusion.1.both), channel_id=1, source_target_pairs={{0,1},{1,0},{2,3},{3,2},{4,5},{5,4},{6,7},{7,6},{8,9},{9,8},{10,11... | collective-permute-start | bytes 3538952 | tf_op jit(solution)/shard_map/ppermute | solution.py:29
  73.5 31.6 %collective-permute-start.15 = (bf16[2,4,48,1536]{3,2,1,0:T(8,128)(2,1)}, bf16[2,4,48,1536]{3,2,1,0:T(8,128)(2,1)}, u32[]{:S(2)}, u32[]{:S(2)}) collective-permute-start(bf16[2,4,48,1536]{3,2,1,0:T(8,128)(2,1)} %collective-permute-done.13.distant), channel_id=1, source_target_pairs={{0,1},{1,0},{2,3},{3,2},{4,5},{5,4},{6,7},{7,6},{8,9},{9,8},{10,11... | collective-permute-start | bytes 3538952 | tf_op jit(solution)/shard_map/ppermute | solution.py:29
  74.7 11.8 collective-permute-start.18
  104.1 314.7 %collective-permute-start.21 = (bf16[2,4,192,384]{3,2,1,0:T(8,128)(2,1)}, bf16[2,4,192,384]{3,2,1,0:T(8,128)(2,1)}, u32[]{:S(2)}, u32[]{:S(2)}) collective-permute-start(bf16[2,4,192,384]{3,2,1,0:T(8,128)(2,1)} %pad_maximum_fusion.2.both), channel_id=1, source_target_pairs={{0,2},{1,5},{2,0},{3,7},{4,6},{5,1},{6,4},{7,3},{8,10},{9,13},{10,... | collective-permute-start | bytes 3538952 | tf_op jit(solution)/shard_map/ppermute | solution.py:29
  105.1 317.7 %collective-permute-start.22 = (bf16[2,4,192,384]{3,2,1,0:T(8,128)(2,1)}, bf16[2,4,192,384]{3,2,1,0:T(8,128)(2,1)}, u32[]{:S(2)}, u32[]{:S(2)}) collective-permute-start(bf16[2,4,192,384]{3,2,1,0:T(8,128)(2,1)} %pad_maximum_fusion.2.both), channel_id=1, source_target_pairs={{0,1},{1,0},{2,3},{3,2},{4,5},{5,4},{6,7},{7,6},{8,9},{9,8},{10,11... | collective-permute-start | bytes 3538952 | tf_op jit(solution)/shard_map/ppermute | solution.py:29
  868.2 334.7 %collective-permute-start.25 = (bf16[2,2,4,48,1536]{4,3,2,1,0:T(8,128)(2,1)}, bf16[2,2,4,48,1536]{4,3,2,1,0:T(8,128)(2,1)}, u32[]{:S(2)}, u32[]{:S(2)}) collective-permute-start(bf16[2,2,4,48,1536]{4,3,2,1,0:T(8,128)(2,1)} %get-tuple-element.81), channel_id=1, source_target_pairs={{0,1},{1,0},{2,3},{3,2},{4,5},{5,4},{6,7},{7,6},{8,9},{9,8},{10,11... | collective-permute-start | bytes 7077896 | tf_op jit(solution)/shard_map/ppermute | solution.py:29
  1023.6 11.2 collective-permute-start.26
  1038.7 162.7 %collective-permute-start.27 = (bf16[2,4,192,384]{3,2,1,0:T(8,128)(2,1)}, bf16[2,4,192,384]{3,2,1,0:T(8,128)(2,1)S(1)}, u32[]{:S(2)}, u32[]{:S(2)}) collective-permute-start(bf16[2,4,192,384]{3,2,1,0:T(8,128)(2,1)} %get-tuple-element.223), channel_id=1, source_target_pairs={{0,2},{1,5},{2,0},{3,7},{4,6},{5,1},{6,4},{7,3},{8,10},{9,13},{10,... | collective-permute-start | bytes 3538952 | tf_op jit(solution)/shard_map/ppermute | solution.py:29
  1201.0 28.4 %collective-permute-start.24 = (bf16[2,2,4,48,1664]{4,3,2,1,0:T(8,128)(2,1)}, bf16[2,2,4,48,1664]{4,3,2,1,0:T(8,128)(2,1)S(1)}, u32[]{:S(2)}, u32[]{:S(2)}) collective-permute-start(bf16[2,2,4,48,1664]{4,3,2,1,0:T(8,128)(2,1)} %get-tuple-element.79), channel_id=1, source_target_pairs={{0,1},{1,0},{2,3},{3,2},{4,5},{5,4},{6,7},{7,6},{8,9},{9,8},{10,11... | collective-permute-start | bytes 7667720 | tf_op jit(solution)/shard_map/ppermute | solution.py:29
  1211.6 16.2 %collective-permute-start.29 = (bf16[2,4,48,1536]{3,2,1,0:T(8,128)(2,1)S(1)}, bf16[2,4,48,1536]{3,2,1,0:T(8,128)(2,1)S(1)}, u32[]{:S(2)}, u32[]{:S(2)}) collective-permute-start(bf16[2,4,48,1536]{3,2,1,0:T(8,128)(2,1)S(1)} %get-tuple-element.84), channel_id=1, source_target_pairs={{0,2},{1,5},{2,0},{3,7},{4,6},{5,1},{6,4},{7,3},{8,10},{9,13},{10,... | collective-permute-start | bytes 3538952 | tf_op jit(solution)/shard_map/ppermute | solution.py:29
  1212.7 17.3 %collective-permute-start.33 = (bf16[192,384]{1,0:T(8,128)(2,1)S(1)}, bf16[192,384]{1,0:T(8,128)(2,1)S(1)}, u32[]{:S(2)}, u32[]{:S(2)}) collective-permute-start(bf16[192,384]{1,0:T(8,128)(2,1)S(1)} %get-tuple-element.235), channel_id=1, source_target_pairs={{0,8},{1,9},{2,10},{3,11},{4,12},{5,13},{6,14},{7,15},{8,0},{9,1},... | collective-permute-start | bytes 442376 | tf_op jit(solution)/shard_map/ppermute | solution.py:29
  1213.1 16.9 %collective-permute-start.34 = (bf16[192,384]{1,0:T(8,128)(2,1)S(1)}, bf16[192,384]{1,0:T(8,128)(2,1)S(1)}, u32[]{:S(2)}, u32[]{:S(2)}) collective-permute-start(bf16[192,384]{1,0:T(8,128)(2,1)S(1)} %get-tuple-element.234), channel_id=1, source_target_pairs={{0,16},{1,17},{2,18},{3,19},{4,20},{5,21},{6,22},{7,23},{8,24},{9,... | collective-permute-start | bytes 442376 | tf_op jit(solution)/shard_map/ppermute | solution.py:29
  1214.7 15.3 %collective-permute-start.35 = (bf16[192,384]{1,0:T(8,128)(2,1)S(1)}, bf16[192,384]{1,0:T(8,128)(2,1)S(1)}, u32[]{:S(2)}, u32[]{:S(2)}) collective-permute-start(bf16[192,384]{1,0:T(8,128)(2,1)S(1)} %get-tuple-element.233), channel_id=1, source_target_pairs={{0,24},{1,25},{2,26},{3,27},{4,28},{5,29},{6,30},{7,31},{8,16},{9,... | collective-permute-start | bytes 442376 | tf_op jit(solution)/shard_map/ppermute | solution.py:29
  1230.2 11.2 collective-permute-start.44
  1238.0 17.5 %collective-permute-start.31 = (bf16[2,4,48,1664]{3,2,1,0:T(8,128)(2,1)S(1)}, bf16[2,4,48,1664]{3,2,1,0:T(8,128)(2,1)S(1)}, u32[]{:S(2)}, u32[]{:S(2)}) collective-permute-start(bf16[2,4,48,1664]{3,2,1,0:T(8,128)(2,1)S(1)} %get-tuple-element.85), channel_id=1, source_target_pairs={{0,2},{1,5},{2,0},{3,7},{4,6},{5,1},{6,4},{7,3},{8,10},{9,13},{10,... | collective-permute-start | bytes 3833864 | tf_op jit(solution)/shard_map/ppermute | solution.py:29
  1242.2 14.7 %collective-permute-start.36 = (bf16[48,1536]{1,0:T(8,128)(2,1)S(1)}, bf16[48,1536]{1,0:T(8,128)(2,1)S(1)}, u32[]{:S(2)}, u32[]{:S(2)}) collective-permute-start(bf16[48,1536]{1,0:T(8,128)(2,1)S(1)} %get-tuple-element.86), channel_id=1, source_target_pairs={{0,8},{1,9},{2,10},{3,11},{4,12},{5,13},{6,14},{7,15},{8,0},{9,1},... | collective-permute-start | bytes 442376 | tf_op jit(solution)/shard_map/ppermute | solution.py:29
  1242.5 14.4 %collective-permute-start.37 = (bf16[48,1536]{1,0:T(8,128)(2,1)S(1)}, bf16[48,1536]{1,0:T(8,128)(2,1)S(1)}, u32[]{:S(2)}, u32[]{:S(2)}) collective-permute-start(bf16[48,1536]{1,0:T(8,128)(2,1)S(1)} %get-tuple-element.87), channel_id=1, source_target_pairs={{0,16},{1,17},{2,18},{3,19},{4,20},{5,21},{6,22},{7,23},{8,24},{9,... | collective-permute-start | bytes 442376 | tf_op jit(solution)/shard_map/ppermute | solution.py:29
  1244.2 12.7 collective-permute-start.38
  1257.0 13.8 %collective-permute-start.43 = (f32[24,1536]{1,0:T(8,128)S(1)}, f32[24,1536]{1,0:T(8,128)S(1)}, u32[]{:S(2)}, u32[]{:S(2)}) collective-permute-start(f32[24,1536]{1,0:T(8,128)S(1)} %slice_select_fusion.4), channel_id=1, source_target_pairs={{0,1},{1,0},{2,3},{3,2},{4,5},{5,4},{6,7},{7,6},{8,9},{9,8},{10,11... | collective-permute-start | bytes 442376 | tf_op jit(solution)/shard_map/ppermute | solution.py:29
  1267.4 11.4 collective-permute-start.40
  1268.2 10.6 collective-permute-start.39
  (260 other events, 5053.7 us)
